TPU v7x, 256 devices: a whole 4x4x8 slice. The times are simulated.
256 devices in a mesh: gx: 4 (over x_lo, core), gy: 8 (over z), gz: 8 (over y, x_hi).
Axes of the slice: x: 4 (x_hi: 2, x_lo: 2; x = x_hi * 2 + x_lo), y: 4, z: 8, core: 2. Of those that a mesh axis runs over, the one named last changes fastest.
Arguments:
- charges: float32 [4, 8, 8, 1024], P('gx', 'gy', 'gz'), may hold values from -6 to 6
- cells: int32 [4, 8, 8, 3, 1024], P('gx', 'gy', 'gz'), may hold values from 0 to 391, as said below
- counts: int32 [4, 8, 8], P('gx', 'gy', 'gz'), may hold values from 128 to 1024, as said below
Outputs:
- potential: float32 [128, 256, 3072], P('gx', 'gy', 'gz')
- forces: float32 [4, 8, 8, 3, 1024], P('gx', 'gy', 'gz')
Inputs may be any that keep to these rules, and one draw needn't show every extreme that they name: `cells`: component 0 lies below 40, component 1 below 40, component 2 below 392. Slots at or past a brick's count are unused. `counts`: some brick holds 1024 atoms.
All inputs are finite; a program needn't handle non-finite values.
Results may differ from a plain program's by a relative error of at most 0.0075.
Values sent between devices are 32-bit elements; how exact they have to be, the bound alone decides.
No kernel may reach another device: no remote copies, remote signals or barrier semaphores. Data moves between devices by JAX's collectives and lax.ppermute only.
A program may use at most 128 MiB of HBM per device.

v0:
```python
import math

import jax
import jax.numpy as jnp
from jax import lax
from jax.experimental import pallas as pl
from jax.experimental.pallas import tpu as pltpu
from jax.sharding import PartitionSpec as P

BX = 32
BY = 32
BZ = 384
A_DEV = 1024
PAD = 4
REACH = 4
WIDTH = A_DEV + 128
BLOCK = 256
SMALL = 128
WIDE = 2 * BLOCK

X0 = 5
Y0 = 8
PX = 42
PY = 48
PZ = 512
CHUNK = 14
FX = 40
FY = 40
FCHUNK = 20

kernel_width = 2.0
EXPONENT = -math.log2(math.e) / (2.0 * kernel_width * kernel_width)
SCALE = 1.3903614627339054
UNIT = math.sqrt(-EXPONENT)
LOW_END = 2 * PAD + 5
HIGH_START = BZ + PAD - 9
HIGH_START_X = BX + PAD - 9
HIGH_START_Y = BY + PAD - 9
MIDDLE = BZ // 2
SPAN = A_DEV + 256 + WIDE
FRONT = 128
MERGED = 9 * A_DEV + SPAN + FRONT
ROWS = FCHUNK * FY


def weight(first, second, scale=1.0):
    away = first - second
    square = away * away
    value = jnp.exp2(math.log2(scale) - square)
    return jnp.where(square < (REACH + 0.5) ** 2 * UNIT * UNIT, value, 0.0)


def iota(shape, dim):
    return lax.broadcasted_iota(jnp.int32, shape, dim).astype(jnp.float32)


def toward(axis):
    return 2 * (lax.axis_index(axis) % 2) - 1


def live_atoms(numbers, charges, cells):
    live = lax.broadcasted_iota(jnp.int32, (1, A_DEV), 1) < numbers[0]
    charge = jnp.where(live, charges[...], 0.0).astype(jnp.bfloat16).astype(jnp.float32)
    places = [jnp.where(live, cells[i], 0) for i in range(3)]
    rows = [charge] + [place.astype(jnp.float32) for place in places[:2]]
    rows.append((places[2] - MIDDLE).astype(jnp.float32))
    rows.append(jnp.zeros((4, A_DEV), jnp.float32))
    return live, places, jnp.concatenate(rows, axis=0).astype(jnp.bfloat16)


def running_sums(masks):
    height = (len(masks) + 7) // 8 * 8
    rows = [jnp.where(mask, 1.0, 0.0) for mask in masks]
    if height > len(masks):
        rows.append(jnp.zeros((height - len(masks), A_DEV), jnp.float32))
    near = jnp.concatenate(rows, axis=0)
    parts = A_DEV // 128
    chunks = jnp.concatenate([near[:, 128 * c : 128 * c + 128] for c in range(parts)], axis=0)
    upto = jnp.where(iota((128, 128), 0) <= iota((128, 128), 1), 1.0, 0.0)
    ahead = jnp.where(iota((A_DEV, 128), 0) < iota((A_DEV, 128), 1) * 128.0, 1.0, 0.0)
    within = jnp.dot(
        chunks.astype(jnp.bfloat16),
        upto.astype(jnp.bfloat16),
        preferred_element_type=jnp.float32,
    )
    before = jnp.dot(
        near.astype(jnp.bfloat16),
        ahead.astype(jnp.bfloat16),
        preferred_element_type=jnp.float32,
    )
    sums = [
        within[height * c : height * (c + 1)] + before[:, c : c + 1] for c in range(parts)
    ]
    return jnp.concatenate(sums, axis=1)


def pick(rows, spot, start, size):
    want = iota((size, A_DEV), 0) + start.astype(jnp.float32)
    hot = jnp.where(want == spot, 1.0, 0.0).astype(jnp.bfloat16)
    return lax.dot_general(
        rows, hot, (((1,), (1,)), ((), ())), preferred_element_type=jnp.float32
    )


def compact(numbers, charges, cells, first, second, lists):
    live, places, rows = live_atoms(numbers, charges, cells)
    depth = places[2]
    masks = [live & (depth < LOW_END), live & (depth >= HIGH_START)]
    sums = running_sums(masks)
    totals = sums[:, A_DEV - 1 : A_DEV]
    spot = [jnp.where(masks[i], sums[i : i + 1] - 1.0, -1.0) for i in range(2)]
    steps = (jnp.max(totals).astype(jnp.int32) + SMALL - 1) // SMALL
    for side in range(2):
        lists[side, :, 0:A_DEV] = jnp.zeros((4, A_DEV), jnp.float32)
        lists[side, :, A_DEV:WIDTH] = jnp.broadcast_to(
            totals[side : side + 1], (4, WIDTH - A_DEV)
        )

    def window(k, _):
        cols = pl.ds(pl.multiple_of(k * SMALL, SMALL), SMALL)
        for side in range(2):
            moved = pick(rows, spot[side], k * SMALL, SMALL)
            lists[side, 0:3, cols] = moved[0:3]
            lists[side, 3:4, cols] = moved[3:4] + float(MIDDLE)
        return 0

    window(jnp.int32(0), 0)
    lax.fori_loop(1, steps, window, 0)
    odd = lax.axis_index("gz") % 2
    first[...] = lists[odd]
    second[...] = lists[1 - odd]


def arrange(numbers, charges, cells, own, first, second, lists):
    live, places, rows = live_atoms(numbers, charges, cells)
    high = live & (places[1] >= HIGH_START_Y)
    low = live & (places[1] < LOW_END)
    sides = [live, live & (places[0] < LOW_END), live & (places[0] >= HIGH_START_X)]
    sums = running_sums([mask for side in sides for mask in (high & side, low & side, side)])
    totals = sums[:, A_DEV - 1 : A_DEV]
    spots = []
    for i, side in enumerate(sides):
        highs, lows, alls = (sums[3 * i + j : 3 * i + j + 1] for j in range(3))
        ends = [totals[3 * i + j : 3 * i + j + 1] for j in range(3)]
        spot = jnp.where(low, ends[2] - ends[1] + lows, ends[0] + alls - highs - lows)
        spot = jnp.where(high, highs, spot) - 1.0
        spots.append(jnp.where(side, spot, -1.0))
        out = own if i == 0 else lists.at[i - 1]
        out[:, 0:A_DEV] = jnp.zeros((4, A_DEV), jnp.float32)
        for row, end in enumerate((2, 0, 1, 2)):
            out[row : row + 1, A_DEV:WIDTH] = jnp.broadcast_to(ends[end], (1, WIDTH - A_DEV))

    def fill(out, spot, k):
        cols = pl.ds(pl.multiple_of(k * BLOCK, BLOCK), BLOCK)
        moved = pick(rows, spot, k * BLOCK, BLOCK)
        out[0:3, cols] = moved[0:3]
        out[3:4, cols] = moved[3:4] + float(MIDDLE)

    def window(k, _):
        fill(own, spots[0], k)
        return 0

    def side_window(k, _):
        fill(lists.at[0], spots[1], k)
        fill(lists.at[1], spots[2], k)
        return 0

    widest = jnp.maximum(jnp.max(totals[5:6]), jnp.max(totals[8:9])).astype(jnp.int32)
    side_window(jnp.int32(0), 0)
    lax.fori_loop(0, (numbers[0] + BLOCK - 1) // BLOCK, window, 0)
    lax.fori_loop(1, (widest + BLOCK - 1) // BLOCK, side_window, 0)
    odd = lax.axis_index("gx") % 2
    first[...] = lists[odd]
    second[...] = lists[1 - odd]


def append(ref, brick, start, number, offset, dx, dy, dz, merged, padded):
    row = lax.broadcasted_iota(jnp.int32, (4, 128), 0)
    moved = jnp.where(row == 1, jnp.float32(X0 - PAD + BX * dx), 0.0)
    moved = jnp.where(row == 2, jnp.float32(Y0 - PAD + BY * dy), moved)
    moved = jnp.where(row == 3, jnp.float32(BZ * dz - PAD), moved)
    unit = jnp.where(row == 0, 1.0, UNIT)
    for c in range(0, A_DEV, 128):
        padded[0:4, c : c + 128] = (ref[brick, :, c : c + 128] + moved) * unit
    skip = start % 128
    atoms = padded[:, pl.ds(pl.multiple_of(start - skip, 128), SPAN)]
    lanes = lax.broadcasted_iota(jnp.int32, (8, SPAN), 1)
    atoms = jnp.where((lanes >= skip) & (lanes < skip + number), atoms, 0.0)
    room = offset % 128
    back = jnp.where(room >= skip, 0, 128)
    atoms = pltpu.roll(atoms, room - skip + back, 1)
    base = pl.multiple_of(FRONT + offset - room - back, 128)
    merged[:, pl.ds(base, 256)] += atoms[:, 0:256]
    merged[:, pl.ds(base + 256, SPAN - 256)] = atoms[:, 256:SPAN]
    return offset + number


def spread(merged, start, size, x0, nx, y0, ny, grid, rows_x, first, row0):
    cols = pl.ds(pl.multiple_of(start + FRONT, 128), size)
    charge = merged[0:1, cols]
    xa = merged[1:2, cols]
    ya = merged[2:3, cols]
    za = merged[3:4, cols]
    gy = weight((iota((ny, size), 0) + jnp.float32(y0)) * UNIT, ya) * (charge * (1.0 / SCALE))
    zi = iota((PZ, size), 0)
    zi = jnp.where(zi < 448.0, zi, zi - float(PZ)) * UNIT
    right = weight(zi, za, SCALE).astype(jnp.bfloat16)
    rows_x[:, 0:size] = weight(iota((48, size), 0) * UNIT, xa)
    chunk = min(nx, CHUNK * PY // ny)
    for c in range(0, nx, chunk):
        at = x0 + c
        left = jnp.stack(
            [rows_x[pl.ds(at + i, 1), 0:size] * gy for i in range(chunk)], axis=0
        )
        left = left.reshape(chunk * ny, size).astype(jnp.bfloat16)
        part = lax.dot_general(
            left, right, (((1,), (1,)), ((), ())), preferred_element_type=jnp.float32
        )
        part = part.reshape(chunk, ny, PZ)
        if first:
            grid[pl.ds(at, chunk), pl.ds(row0, ny), :] = part
        else:
            grid[pl.ds(at, chunk), pl.ds(row0, ny), :] += part


def spread_all(merged, total, x0, nx, y0, ny, grid, rows_x, clear, row0):
    rest = total % WIDE
    wide = total // WIDE + (rest > BLOCK).astype(jnp.int32)

    def put(start, size, first):
        spread(merged, start, size, x0, nx, y0, ny, grid, rows_x, first, row0)

    def block(k, _):
        put(k * WIDE, WIDE, False)
        return 0

    if clear:

        @pl.when(wide > 0)
        def _():
            put(0, WIDE, True)

        @pl.when(wide == 0)
        def _():
            put(0, BLOCK, True)

    lax.fori_loop(1 if clear else 0, wide, block, 0)

    @pl.when(total > (jnp.maximum(wide * WIDE, BLOCK) if clear else wide * WIDE))
    def _():
        put(wide * WIDE, BLOCK, False)


def number_of(ref, brick, row):
    return ref[brick, row : row + 1, A_DEV:WIDTH][0, 0].astype(jnp.int32)


def gather(ref, bricks, side, merged, padded):
    merged[:, 0 : FRONT + 256] = jnp.zeros((8, FRONT + 256), jnp.float32)
    offset = jnp.int32(0)
    for brick, (dx, dy, dz) in bricks:
        number = number_of(ref, brick, 0)
        start = jnp.int32(0)
        if side is not None and type(dz) is int:
            low = number_of(ref, brick, 2)
            start = jnp.where(side > 0, number - low, 0)
            number = jnp.where(side > 0, low, number_of(ref, brick, 1))
        offset = append(ref, brick, start, number, offset, dx, dy, dz, merged, padded)
    return offset


def slots_of(axis):
    step = toward(axis)
    return (step, 0, -step)


def inner(lists, grid, rows_x, merged, padded):
    padded[...] = jnp.zeros_like(padded)
    zs = slots_of("gz")
    total = gather(lists, [(j, (0, 0, zs[j])) for j in (1, 0, 2)], None, merged, padded)
    spread_all(merged, total, 0, PX, 0, PY, grid, rows_x, True, 0)


def column(
    lists, place, before, grid, potential, found, rows_x, fields, merged, padded, sem
):
    padded[...] = jnp.zeros_like(padded)
    xs, zs = slots_of("gx"), slots_of("gz")
    for i in (0, 2):
        total = gather(
            lists, [(3 * i + j, (xs[i], 0, zs[j])) for j in range(3)], None, merged, padded
        )
        x0 = jnp.where(xs[i] > 0, 28, 0)
        spread_all(merged, total, x0, 14, 0, PY, grid, rows_x, False, 0)
    copy = pltpu.make_async_copy(
        grid.at[X0 : X0 + BX, 16:32, 0:BZ], potential.at[:, 8:24, :], sem
    )
    copy.start()
    found[...] = jnp.zeros_like(found)
    count = number_of(lists, 4, 0)

    def build(c):
        gx, gy, gz = [], [], []
        for x in range(c * FCHUNK, (c + 1) * FCHUNK):
            gx.append(grid[x + 2, 4:44, :] - grid[x, 4:44, :])
            gy.append(grid[x + 1, 5:45, :] - grid[x + 1, 3:43, :])
            mid = grid[x + 1, 4:44, :]
            gz.append(pltpu.roll(mid, PZ - 2, 1) - mid)
        for d, parts in enumerate((gx, gy, gz)):
            both = jnp.stack(parts, axis=0).reshape(ROWS, PZ).astype(jnp.bfloat16)
            fields[d, c * ROWS : (c + 1) * ROWS, :] = both

    def sample(start, fresh):
        cols = pl.ds(pl.multiple_of(start, WIDE), WIDE)
        xa, ya, za = atom_cells(place, cols)
        zi = depths(WIDE)
        depth = jnp.where(zi == za, 1.0, 0.0).astype(jnp.bfloat16)
        below = jnp.where(zi == za - 1.0, 1.0, 0.0).astype(jnp.bfloat16)
        sums = [jnp.zeros((FY, WIDE), jnp.float32)] * 3
        for c in range(FX // FCHUNK):
            if fresh:
                build(c)
            for d in range(3):
                part = jnp.dot(
                    fields[d, c * ROWS : (c + 1) * ROWS, :],
                    below if d == 2 else depth,
                    preferred_element_type=jnp.float32,
                ).reshape(FCHUNK, FY, WIDE)
                for i in range(FCHUNK):
                    hot_x = xa == float(c * FCHUNK + i)
                    sums[d] = sums[d] + jnp.where(hot_x, part[i], 0.0)
        hot_y = iota((FY, WIDE), 0) == ya
        for d in range(3):
            value = jnp.sum(jnp.where(hot_y, sums[d], 0.0), axis=0, keepdims=True)
            found[d : d + 1, cols] = value

    sample(0, True)

    def more(k, _):
        sample(k * WIDE, False)
        return 0

    lax.fori_loop(1, (count + WIDE - 1) // WIDE, more, 0)
    copy.wait()


def atom_cells(place, cols):
    xa = place[0, :, cols].astype(jnp.float32)
    ya = place[1, :, cols].astype(jnp.float32)
    return xa, ya, (place[2, :, cols] - PAD).astype(jnp.float32)


def depths(size):
    zi = iota((PZ, size), 0)
    return jnp.where(zi < 448.0, zi, zi - float(PZ))


def slab(turn, lists, grid, potential, part, stage, rows_x, merged, padded, sem):
    xs, zs = slots_of("gx"), slots_of("gz")
    dy = toward("gy") * turn
    total = gather(
        lists,
        [(3 * m + j, (xs[m], dy, zs[j])) for m in range(3) for j in range(3)],
        dy,
        merged,
        padded,
    )
    y0 = pl.multiple_of(jnp.where(dy > 0, 32, 0), 8)
    spread_all(merged, total, 0, PX, y0, 16, part, rows_x, True, 0)
    at = pl.multiple_of(jnp.where(dy > 0, 0, 8), 8)
    stage[...] = (
        part[X0 : X0 + BX, pl.ds(at, 8), 0:BZ] + grid[X0 : X0 + BX, pl.ds(y0 + at, 8), 0:BZ]
    )
    row = pl.multiple_of(jnp.where(dy > 0, 24, 0), 8)
    copy = pltpu.make_async_copy(stage, potential.at[:, pl.ds(row, 8), :], sem)
    copy.start()
    return y0, copy


def finish(
    near, far, own, place, charge, grid, found, potential_in, potential, forces,
    parts, stages, rows_x, merged, padded, sems,
):
    padded[...] = jnp.zeros_like(padded)
    slabs = [
        slab(
            1 - 2 * i, lists, grid, potential, parts.at[i], stages.at[i],
            rows_x, merged, padded, sems.at[i],
        )
        for i, lists in enumerate((near, far))
    ]
    count = number_of(own, 0, 0)
    forces[...] = jnp.zeros_like(forces)

    def block(k, _):
        cols = pl.ds(pl.multiple_of(k * WIDE, WIDE), WIDE)
        xa, ya, za = atom_cells(place, cols)
        zi = depths(WIDE)
        here = jnp.where(zi == za, 1.0, 0.0).astype(jnp.bfloat16)
        slope = jnp.where(zi == za + 1.0, 1.0, 0.0) - jnp.where(zi == za - 1.0, 1.0, 0.0)
        slope = slope.astype(jnp.bfloat16)
        sums = [found[d : d + 1, cols] for d in range(3)]
        for i, (y0, _) in enumerate(slabs):
            rows = parts[i].reshape(PX * 16, PZ).astype(jnp.bfloat16)
            value = jnp.dot(rows, here, preferred_element_type=jnp.float32)
            value = value.reshape(PX, 16, WIDE)
            change = jnp.dot(rows, slope, preferred_element_type=jnp.float32)
            change = change.reshape(PX, 16, WIDE)
            level = jnp.zeros((16, WIDE), jnp.float32)
            along_x = level
            along_z = level
            for x in range(PX):
                at_x = xa == float(x - 1)
                level = level + jnp.where(at_x, value[x], 0.0)
                along_z = along_z + jnp.where(at_x, change[x], 0.0)
                side = jnp.where(xa == float(x - 2), 1.0, 0.0)
                side = side - jnp.where(xa == float(x), 1.0, 0.0)
                along_x = along_x + side * value[x]
            away = iota((16, WIDE), 0) + (y0.astype(jnp.float32) - float(Y0 - PAD)) - ya
            at_y = away == 0.0
            fx = jnp.where(at_y, along_x, 0.0)
            fy = jnp.where(away == 1.0, level, 0.0) - jnp.where(away == -1.0, level, 0.0)
            fz = jnp.where(at_y, along_z, 0.0)
            for d, one in enumerate((fx, fy, fz)):
                sums[d] = sums[d] + jnp.sum(one, axis=0, keepdims=True)
        slots = lax.broadcasted_iota(jnp.int32, (1, WIDE), 1) + k * WIDE
        factor = -0.5 * charge[:, cols]
        for d in range(3):
            forces[d, :, cols] = jnp.where(slots < count, sums[d] * factor, 0.0)
        return 0

    lax.fori_loop(0, (count + WIDE - 1) // WIDE, block, 0)
    for _, copy in slabs:
        copy.wait()


def swaps(block, other, axis):
    size = lax.axis_size(axis)
    first = [(i, (i + 1 if i % 2 else i - 1) % size) for i in range(size)]
    second = [(i, i ^ 1) for i in range(size)]
    return lax.ppermute(block, axis, first), lax.ppermute(other, axis, second)


VMEM = pl.BlockSpec(memory_space=pltpu.VMEM)
HBM = pl.BlockSpec(memory_space=pl.ANY)
LIMIT = 40 * 1024 * 1024


def call_compact(counts, charge, cells):
    shape = pltpu.VMEM((4, WIDTH), jnp.float32)
    return pl.pallas_call(
        compact,
        out_shape=(shape, shape),
        in_specs=[pl.BlockSpec(memory_space=pltpu.SMEM), VMEM, VMEM],
        out_specs=(VMEM,) * 2,
        scratch_shapes=[pltpu.VMEM((2, 4, WIDTH), jnp.float32)],
    )(counts, charge, cells)


def call_arrange(counts, charge, cells):
    shape = pltpu.VMEM((4, WIDTH), jnp.float32)
    return pl.pallas_call(
        arrange,
        out_shape=(shape, shape, shape),
        in_specs=[pl.BlockSpec(memory_space=pltpu.SMEM), VMEM, VMEM],
        out_specs=(VMEM,) * 3,
        scratch_shapes=[pltpu.VMEM((2, 4, WIDTH), jnp.float32)],
        cost_estimate=pl.CostEstimate(flops=2 * 10**9, bytes_accessed=10**5, transcendentals=0),
    )(counts, charge, cells)


GRID = pltpu.VMEM((PX, PY, PZ), jnp.float32)
FOUND = pltpu.VMEM((8, A_DEV), jnp.float32)
ROWS_X = pltpu.VMEM((48, WIDE), jnp.float32)
LISTS = [
    pltpu.VMEM((8, MERGED), jnp.float32),
    pltpu.VMEM((8, A_DEV + SPAN), jnp.float32),
]
PARAMS = pltpu.CompilerParams(vmem_limit_bytes=LIMIT)


def cost(flops):
    return pl.CostEstimate(flops=flops, bytes_accessed=10**6, transcendentals=0)


def call_inner(lists):
    return pl.pallas_call(
        inner,
        out_shape=GRID,
        in_specs=[VMEM],
        out_specs=VMEM,
        scratch_shapes=[ROWS_X] + LISTS,
        compiler_params=PARAMS,
        cost_estimate=cost(2 * 10**9),
    )(lists)


def call_column(lists, cells, grid):
    return pl.pallas_call(
        column,
        out_shape=(GRID, jax.ShapeDtypeStruct((BX, BY, BZ), jnp.float32), FOUND),
        in_specs=[VMEM, VMEM, VMEM],
        out_specs=(VMEM, HBM, VMEM),
        input_output_aliases={2: 0},
        scratch_shapes=[ROWS_X, pltpu.VMEM((3, FX * FY, PZ), jnp.bfloat16)]
        + LISTS
        + [pltpu.SemaphoreType.DMA],
        compiler_params=PARAMS,
        cost_estimate=cost(6 * 10**9),
    )(lists, cells, grid)


def call_finish(near, far, own, cells, charge, grid, found, potential):
    return pl.pallas_call(
        finish,
        out_shape=(
            jax.ShapeDtypeStruct((BX, BY, BZ), jnp.float32),
            jax.ShapeDtypeStruct((3, 1, A_DEV), jnp.float32),
        ),
        in_specs=[VMEM] * 7 + [HBM],
        out_specs=(HBM, VMEM),
        input_output_aliases={7: 0},
        scratch_shapes=[
            pltpu.VMEM((2, PX, 16, PZ), jnp.float32),
            pltpu.VMEM((2, BX, 8, BZ), jnp.float32),
            ROWS_X,
        ]
        + LISTS
        + [pltpu.SemaphoreType.DMA((2,))],
        compiler_params=PARAMS,
    )(near, far, own, cells, charge, grid, found, potential)


def local(charges, cells, counts):
    charge = charges.reshape(1, A_DEV)
    cells = cells.reshape(3, 1, A_DEV)
    counts = counts.reshape(1)
    first, second = call_compact(counts, charge, cells)
    own, to_first, to_second = call_arrange(counts, charge, cells)
    own = own[None]
    first, second = swaps(first[None], second[None], "gz")
    atoms, to_first, to_second = (
        jnp.concatenate([first, middle, second], axis=0)
        for middle in (own, to_first[None], to_second[None])
    )
    first, second = swaps(to_first, to_second, "gx")
    grid = call_inner(atoms)
    atoms = jnp.concatenate([first, atoms, second], axis=0)
    first, second = swaps(atoms, atoms, "gy")
    grid, potential, found = call_column(atoms, cells, grid)
    potential, forces = call_finish(first, second, own, cells, charge, grid, found, potential)
    return potential, forces.reshape(1, 1, 1, 3, A_DEV)


def solution(mesh):
    in_specs = (P("gx", "gy", "gz", None), P("gx", "gy", "gz", None, None), P("gx", "gy", "gz"))
    out_specs = (P("gx", "gy", "gz"), P("gx", "gy", "gz", None, None))
    return jax.shard_map(local, mesh=mesh, in_specs=in_specs, out_specs=out_specs, check_vma=False)
```

profile of v0, /device:TPU:2, one launch (start us, length us, event | category | flops | bytes accessed | tf_op | source)
XLA Modules:
  0.0 32.9 jit_solution(4009518582134072792)
XLA Ops:
  1.3 1.3 %shard_map.50 = (f32[4,1152]{1,0:T(4,128)S(1)}, f32[4,1152]{1,0:T(4,128)S(1)}) custom-call(s32[1]{0:T(128)} %bitcast.12.numbers, f32[1,1024]{1,0:T(1,128)} %bitcast.22, s32[3,1,1024]{2,1,0:T(1,128)} %bitcast.16), custom_call_target="tpu_custom_call" | custom-call | tf_op jit(solution)/shard_map/pallas_call | solution.py:451
  2.5 4.6 %collective-permute-start = (f32[1,4,1152]{2,1,0:T(4,128)S(1)}, f32[1,4,1152]{2,1,0:T(4,128)S(1)}, u32[]{:S(2)}, u32[]{:S(2)}) collective-permute-start(f32[1,4,1152]{2,1,0:T(4,128)S(1)} %bitcast.26), channel_id=1, source_target_pairs={{0,7},{1,2},{2,1},{3,4},{4,3},{5,6},{6,5},{7,0},{8,15},{9,10},{10,... | collective-permute-start | bytes 55304 | tf_op jit(solution)/shard_map/ppermute | solution.py:441
  7.1 0.0 collective-permute-start.1
  7.1 1.8 %shard_map.51 = (f32[4,1152]{1,0:T(4,128)S(1)}, f32[4,1152]{1,0:T(4,128)S(1)}, f32[4,1152]{1,0:T(4,128)S(1)}) custom-call(s32[1]{0:T(128)} %bitcast.13.numbers, f32[1,1024]{1,0:T(1,128)} %bitcast.23, s32[3,1,1024]{2,1,0:T(1,128)} %bitcast.17), custom_call_target="tpu_custom_call" | custom-call | flops 2000000000 | bytes 100000 | tf_op jit(solution)/shard_map/pallas_call | solution.py:462
  8.9 0.0 copy-start
  8.9 1.0 %collective-permute-done = f32[1,4,1152]{2,1,0:T(4,128)S(1)} collective-permute-done((f32[1,4,1152]{2,1,0:T(4,128)S(1)}, f32[1,4,1152]{2,1,0:T(4,128)S(1)}, u32[]{:S(2)}, u32[]{:S(2)}) %collective-permute-start) | collective-permute-done | bytes 18464 | tf_op jit(solution)/shard_map/ppermute | solution.py:441
  9.9 2.5 %collective-permute-done.1 = f32[1,4,1152]{2,1,0:T(4,128)S(1)} collective-permute-done((f32[1,4,1152]{2,1,0:T(4,128)S(1)}, f32[1,4,1152]{2,1,0:T(4,128)S(1)}, u32[]{:S(2)}, u32[]{:S(2)}) %collective-permute-start.1) | collective-permute-done | bytes 18464 | tf_op jit(solution)/shard_map/ppermute | solution.py:441
  12.4 0.1 collective-permute-start.2
  12.5 1.5 %collective-permute-start.3 = (f32[3,4,1152]{2,1,0:T(4,128)S(1)}, f32[3,4,1152]{2,1,0:T(4,128)S(1)}, u32[]{:S(2)}, u32[]{:S(2)}) collective-permute-start(f32[3,4,1152]{2,1,0:T(4,128)S(1)} %get-tuple-element.25), channel_id=1, source_target_pairs={{0,64},{64,0},{128,192},{192,128},{1,65},{65,1},{129,193},{193,129... | collective-permute-start | bytes 165896 | tf_op jit(solution)/shard_map/ppermute | solution.py:441
  14.1 1.0 %shard_map.52.before = f32[42,48,512]{2,1,0:T(8,128)S(1)} custom-call(f32[3,4,1152]{2,1,0:T(4,128)S(1)} %get-tuple-element.24.lists), custom_call_target="tpu_custom_call" | custom-call | flops 2000000000 | bytes 1000000 | tf_op jit(solution)/shard_map/pallas_call | solution.py:487
  15.1 1.6 %collective-permute-done.2 = f32[3,4,1152]{2,1,0:T(4,128)S(1)} collective-permute-done((f32[3,4,1152]{2,1,0:T(4,128)S(1)}, f32[3,4,1152]{2,1,0:T(4,128)S(1)}, u32[]{:S(2)}, u32[]{:S(2)}) %collective-permute-start.2) | collective-permute-done | bytes 55328 | tf_op jit(solution)/shard_map/ppermute | solution.py:441
  16.7 0.0 collective-permute-done.3
  16.7 0.0 copy-start.1
  16.8 5.9 %collective-permute-start.4 = (f32[9,4,1152]{2,1,0:T(4,128)S(1)}, f32[9,4,1152]{2,1,0:T(4,128)S(1)}, u32[]{:S(2)}, u32[]{:S(2)}) collective-permute-start(f32[9,4,1152]{2,1,0:T(4,128)S(1)} %constant_dynamic-update-slice_fusion.lists), channel_id=1, source_target_pairs={{0,56},{8,16},{16,8},{24,32},{32,24},{40,48},{48,40},{56,0},{1,57}... | collective-permute-start | bytes 497672 | tf_op jit(solution)/shard_map/ppermute | solution.py:441
  22.7 0.0 collective-permute-start.5
  22.7 0.0 copy-done
  22.7 5.3 %shard_map.53 = (f32[42,48,512]{2,1,0:T(8,128)S(1)}, f32[32,32,384]{2,1,0:T(8,128)}, f32[8,1024]{1,0:T(8,128)S(1)}) custom-call(f32[9,4,1152]{2,1,0:T(4,128)S(1)} %constant_dynamic-update-slice_fusion.lists, s32[3,1,1024]{2,1,0:T(1,128)S(1)} %bitcast.18, f32[42,48,512]{2,1,0:T(8,128)S(1)} %shard_map.52.before), custom_call_target="tpu_custom_call", output_to_operand_aliasing={{0}: (2, {})} | custom-call | flops 6000000000 | bytes 1000000 | tf_op jit(solution)/shard_map/pallas_call | solution.py:499
  28.0 0.0 collective-permute-done.4.near
  28.0 0.6 %collective-permute-done.5.far = f32[9,4,1152]{2,1,0:T(4,128)S(1)} collective-permute-done((f32[9,4,1152]{2,1,0:T(4,128)S(1)}, f32[9,4,1152]{2,1,0:T(4,128)S(1)}, u32[]{:S(2)}, u32[]{:S(2)}) %collective-permute-start.5) | collective-permute-done | bytes 165920 | tf_op jit(solution)/shard_map/ppermute | solution.py:441
  28.7 0.0 copy-done.1
  28.7 4.1 %shard_map.54 = (f32[32,32,384]{2,1,0:T(8,128)}, f32[3,1,1024]{2,1,0:T(1,128)}) custom-call(f32[9,4,1152]{2,1,0:T(4,128)S(1)} %collective-permute-done.4.near, f32[9,4,1152]{2,1,0:T(4,128)S(1)} %collective-permute-done.5.far, f32[1,4,1152]{2,1,0:T(4,128)S(1)} %bitcast.15, s32[3,1,1024]{2,1,0:T(1,128)S(1)} %bitcast.19, ...), custom_call_target="tpu_custom_call", output_to_operand_aliasing={{0}: (7, {})} | custom-call | tf_op jit(solution)/shard_map/pallas_call | solution.py:514
  (6 shorter events, 0.1 us)
Async XLA Ops:
  2.5 7.4 %collective-permute-start = (f32[1,4,1152]{2,1,0:T(4,128)S(1)}, f32[1,4,1152]{2,1,0:T(4,128)S(1)}, u32[]{:S(2)}, u32[]{:S(2)}) collective-permute-start(f32[1,4,1152]{2,1,0:T(4,128)S(1)} %bitcast.26), channel_id=1, source_target_pairs={{0,7},{1,2},{2,1},{3,4},{4,3},{5,6},{6,5},{7,0},{8,15},{9,10},{10,... | collective-permute-start | bytes 55304 | tf_op jit(solution)/shard_map/ppermute | solution.py:441
  7.1 5.3 %collective-permute-start.1 = (f32[1,4,1152]{2,1,0:T(4,128)S(1)}, f32[1,4,1152]{2,1,0:T(4,128)S(1)}, u32[]{:S(2)}, u32[]{:S(2)}) collective-permute-start(f32[1,4,1152]{2,1,0:T(4,128)S(1)} %bitcast.25), channel_id=1, source_target_pairs={{0,1},{1,0},{2,3},{3,2},{4,5},{5,4},{6,7},{7,6},{8,9},{9,8},{10,11... | collective-permute-start | bytes 55304 | tf_op jit(solution)/shard_map/ppermute | solution.py:441
  8.9 13.8 %copy-start = (s32[1,1,1,3,1024]{4,2,3,1,0:T(1,128)S(1)}, s32[1,1,1,3,1024]{4,2,3,1,0:T(1,128)}, u32[]{:S(2)}) copy-start(s32[1,1,1,3,1024]{4,2,3,1,0:T(1,128)} %param.4) | copy-start | bytes 36868
  12.4 4.2 %collective-permute-start.2 = (f32[3,4,1152]{2,1,0:T(4,128)S(1)}, f32[3,4,1152]{2,1,0:T(4,128)S(1)}, u32[]{:S(2)}, u32[]{:S(2)}) collective-permute-start(f32[3,4,1152]{2,1,0:T(4,128)S(1)} %get-tuple-element.26), channel_id=1, source_target_pairs={{0,192},{64,128},{128,64},{192,0},{1,193},{65,129},{129,65},{193,1... | collective-permute-start | bytes 165896 | tf_op jit(solution)/shard_map/ppermute | solution.py:441
  12.5 4.2 %collective-permute-start.3 = (f32[3,4,1152]{2,1,0:T(4,128)S(1)}, f32[3,4,1152]{2,1,0:T(4,128)S(1)}, u32[]{:S(2)}, u32[]{:S(2)}) collective-permute-start(f32[3,4,1152]{2,1,0:T(4,128)S(1)} %get-tuple-element.25), channel_id=1, source_target_pairs={{0,64},{64,0},{128,192},{192,128},{1,65},{65,1},{129,193},{193,129... | collective-permute-start | bytes 165896 | tf_op jit(solution)/shard_map/ppermute | solution.py:441
  16.7 11.9 %copy-start.1 = (f32[1,1,1,1024]{3,2,1,0:T(1,128)S(1)}, f32[1,1,1,1024]{3,2,1,0:T(1,128)}, u32[]{:S(2)}) copy-start(f32[1,1,1,1024]{3,2,1,0:T(1,128)} %param.3) | copy-start | bytes 12292
  16.8 11.3 %collective-permute-start.4 = (f32[9,4,1152]{2,1,0:T(4,128)S(1)}, f32[9,4,1152]{2,1,0:T(4,128)S(1)}, u32[]{:S(2)}, u32[]{:S(2)}) collective-permute-start(f32[9,4,1152]{2,1,0:T(4,128)S(1)} %constant_dynamic-update-slice_fusion.lists), channel_id=1, source_target_pairs={{0,56},{8,16},{16,8},{24,32},{32,24},{40,48},{48,40},{56,0},{1,57}... | collective-permute-start | bytes 497672 | tf_op jit(solution)/shard_map/ppermute | solution.py:441
  22.7 6.0 %collective-permute-start.5 = (f32[9,4,1152]{2,1,0:T(4,128)S(1)}, f32[9,4,1152]{2,1,0:T(4,128)S(1)}, u32[]{:S(2)}, u32[]{:S(2)}) collective-permute-start(f32[9,4,1152]{2,1,0:T(4,128)S(1)} %constant_dynamic-update-slice_fusion.lists), channel_id=1, source_target_pairs={{0,8},{8,0},{16,24},{24,16},{32,40},{40,32},{48,56},{56,48},{1,9},... | collective-permute-start | bytes 497672 | tf_op jit(solution)/shard_map/ppermute | solution.py:441
where the time goes:
time: 33.3 us; the launch traced here: 32.9 us
  Pallas kernels  13.5 us (41%)
  starting transfers between devices  12.2 us (37%)
  waiting for transfers between devices  5.68 us (17%)
  between operations  1.52 us (5%)
    ppermute x6, starting transfers between devices, swaps(): return (lax.ppermute(block, axis, first), lax.ppermute(other, axis, second))  12.2 us
    ppermute x6, waiting for transfers between devices, swaps(): return (lax.ppermute(block, axis, first), lax.ppermute(other, axis, second))  5.68 us
    pallas_call x1, Pallas kernels, call_column(): pl.pallas_call(column, out_shape=(GRID, jax.ShapeDtypeStruct((BX, BY, BZ)...  5.31 us
    pallas_call x1, Pallas kernels, call_finish(): pl.pallas_call(finish, out_shape=(jax.ShapeDtypeStruct((BX, BY, BZ), jnp....  4.09 us
    pallas_call x1, Pallas kernels, call_arrange(): pl.pallas_call(arrange, out_shape=(shape, shape, shape), in_specs=[pl.Blo...  1.78 us
    pallas_call x1, Pallas kernels, call_compact(): pl.pallas_call(compact, out_shape=(shape, shape), in_specs=[pl.BlockSpec(...  1.25 us
    pallas_call x1, Pallas kernels, call_inner(): pl.pallas_call(inner, out_shape=GRID, in_specs=[VMEM], out_specs=VMEM, sc...  1.03 us
  transfers between devices with their start and end apart: 6, of which 4 were waited for; matrix products, arithmetic and copies ran while one was open for 0% of the time, Pallas kernels for 25%

commit v1 on v0

--- a/solution.py
+++ b/solution.py
@@ -23,10 +23,10 @@
 PX = 42
 PY = 48
 PZ = 512
-CHUNK = 14
+CHUNK = 42
 FX = 40
 FY = 40
-FCHUNK = 20
+FCHUNK = 10
 
 kernel_width = 2.0
 EXPONENT = -math.log2(math.e) / (2.0 * kernel_width * kernel_width)

time: 33.3 us -> 33.8 us (1.015)
  no operation moved by 1% of the time
where the time goes in v1:
time: 33.8 us; the launch traced here: 33.1 us
  Pallas kernels  13.7 us (41%)
  starting transfers between devices  12.2 us (36%)
  waiting for transfers between devices  5.65 us (17%)
  between operations  1.52 us (4%)
    ppermute x6, starting transfers between devices, swaps(): return (lax.ppermute(block, axis, first), lax.ppermute(other, axis, second))  12.2 us
    ppermute x6, waiting for transfers between devices, swaps(): return (lax.ppermute(block, axis, first), lax.ppermute(other, axis, second))  5.65 us
    pallas_call x1, Pallas kernels, call_column(): pl.pallas_call(column, out_shape=(GRID, jax.ShapeDtypeStruct((BX, BY, BZ)...  5.37 us
    pallas_call x1, Pallas kernels, call_finish(): pl.pallas_call(finish, out_shape=(jax.ShapeDtypeStruct((BX, BY, BZ), jnp....  4.32 us
    pallas_call x1, Pallas kernels, call_arrange(): pl.pallas_call(arrange, out_shape=(shape, shape, shape), in_specs=[pl.Blo...  1.78 us
    pallas_call x1, Pallas kernels, call_compact(): pl.pallas_call(compact, out_shape=(shape, shape), in_specs=[pl.BlockSpec(...  1.25 us
    pallas_call x1, Pallas kernels, call_inner(): pl.pallas_call(inner, out_shape=GRID, in_specs=[VMEM], out_specs=VMEM, sc...  1 us
  transfers between devices with their start and end apart: 6, of which 4 were waited for; matrix products, arithmetic and copies ran while one was open for 0% of the time, Pallas kernels for 25%

profile of v1, /device:TPU:2, one launch (start us, length us, event | category | flops | bytes accessed | tf_op | source)
XLA Modules:
  0.0 33.1 jit_solution(12879750787635517314)
XLA Ops:
  1.3 1.3 %shard_map.50 = (f32[4,1152]{1,0:T(4,128)S(1)}, f32[4,1152]{1,0:T(4,128)S(1)}) custom-call(s32[1]{0:T(128)} %bitcast.12.numbers, f32[1,1024]{1,0:T(1,128)} %bitcast.22, s32[3,1,1024]{2,1,0:T(1,128)} %bitcast.16), custom_call_target="tpu_custom_call" | custom-call | tf_op jit(solution)/shard_map/pallas_call | solution.py:451
  2.5 4.6 %collective-permute-start = (f32[1,4,1152]{2,1,0:T(4,128)S(1)}, f32[1,4,1152]{2,1,0:T(4,128)S(1)}, u32[]{:S(2)}, u32[]{:S(2)}) collective-permute-start(f32[1,4,1152]{2,1,0:T(4,128)S(1)} %bitcast.26), channel_id=1, source_target_pairs={{0,7},{1,2},{2,1},{3,4},{4,3},{5,6},{6,5},{7,0},{8,15},{9,10},{10,... | collective-permute-start | bytes 55304 | tf_op jit(solution)/shard_map/ppermute | solution.py:441
  7.1 0.0 collective-permute-start.1
  7.1 1.8 %shard_map.51 = (f32[4,1152]{1,0:T(4,128)S(1)}, f32[4,1152]{1,0:T(4,128)S(1)}, f32[4,1152]{1,0:T(4,128)S(1)}) custom-call(s32[1]{0:T(128)} %bitcast.13.numbers, f32[1,1024]{1,0:T(1,128)} %bitcast.23, s32[3,1,1024]{2,1,0:T(1,128)} %bitcast.17), custom_call_target="tpu_custom_call" | custom-call | flops 2000000000 | bytes 100000 | tf_op jit(solution)/shard_map/pallas_call | solution.py:462
  8.9 0.0 copy-start
  8.9 1.0 %collective-permute-done = f32[1,4,1152]{2,1,0:T(4,128)S(1)} collective-permute-done((f32[1,4,1152]{2,1,0:T(4,128)S(1)}, f32[1,4,1152]{2,1,0:T(4,128)S(1)}, u32[]{:S(2)}, u32[]{:S(2)}) %collective-permute-start) | collective-permute-done | bytes 18464 | tf_op jit(solution)/shard_map/ppermute | solution.py:441
  9.9 2.5 %collective-permute-done.1 = f32[1,4,1152]{2,1,0:T(4,128)S(1)} collective-permute-done((f32[1,4,1152]{2,1,0:T(4,128)S(1)}, f32[1,4,1152]{2,1,0:T(4,128)S(1)}, u32[]{:S(2)}, u32[]{:S(2)}) %collective-permute-start.1) | collective-permute-done | bytes 18464 | tf_op jit(solution)/shard_map/ppermute | solution.py:441
  12.4 0.1 collective-permute-start.2
  12.5 1.5 %collective-permute-start.3 = (f32[3,4,1152]{2,1,0:T(4,128)S(1)}, f32[3,4,1152]{2,1,0:T(4,128)S(1)}, u32[]{:S(2)}, u32[]{:S(2)}) collective-permute-start(f32[3,4,1152]{2,1,0:T(4,128)S(1)} %get-tuple-element.25), channel_id=1, source_target_pairs={{0,64},{64,0},{128,192},{192,128},{1,65},{65,1},{129,193},{193,129... | collective-permute-start | bytes 165896 | tf_op jit(solution)/shard_map/ppermute | solution.py:441
  14.1 1.0 %shard_map.52.before = f32[42,48,512]{2,1,0:T(8,128)S(1)} custom-call(f32[3,4,1152]{2,1,0:T(4,128)S(1)} %get-tuple-element.24.lists), custom_call_target="tpu_custom_call" | custom-call | flops 2000000000 | bytes 1000000 | tf_op jit(solution)/shard_map/pallas_call | solution.py:487
  15.1 1.6 %collective-permute-done.2 = f32[3,4,1152]{2,1,0:T(4,128)S(1)} collective-permute-done((f32[3,4,1152]{2,1,0:T(4,128)S(1)}, f32[3,4,1152]{2,1,0:T(4,128)S(1)}, u32[]{:S(2)}, u32[]{:S(2)}) %collective-permute-start.2) | collective-permute-done | bytes 55328 | tf_op jit(solution)/shard_map/ppermute | solution.py:441
  16.7 0.0 collective-permute-done.3
  16.7 0.0 copy-start.1
  16.8 5.9 %collective-permute-start.4 = (f32[9,4,1152]{2,1,0:T(4,128)S(1)}, f32[9,4,1152]{2,1,0:T(4,128)S(1)}, u32[]{:S(2)}, u32[]{:S(2)}) collective-permute-start(f32[9,4,1152]{2,1,0:T(4,128)S(1)} %constant_dynamic-update-slice_fusion.lists), channel_id=1, source_target_pairs={{0,56},{8,16},{16,8},{24,32},{32,24},{40,48},{48,40},{56,0},{1,57}... | collective-permute-start | bytes 497672 | tf_op jit(solution)/shard_map/ppermute | solution.py:441
  22.7 0.0 collective-permute-start.5
  22.7 0.0 copy-done
  22.7 5.4 %shard_map.53 = (f32[42,48,512]{2,1,0:T(8,128)S(1)}, f32[32,32,384]{2,1,0:T(8,128)}, f32[8,1024]{1,0:T(8,128)S(1)}) custom-call(f32[9,4,1152]{2,1,0:T(4,128)S(1)} %constant_dynamic-update-slice_fusion.lists, s32[3,1,1024]{2,1,0:T(1,128)S(1)} %bitcast.18, f32[42,48,512]{2,1,0:T(8,128)S(1)} %shard_map.52.before), custom_call_target="tpu_custom_call", output_to_operand_aliasing={{0}: (2, {})} | custom-call | flops 6000000000 | bytes 1000000 | tf_op jit(solution)/shard_map/pallas_call | solution.py:499
  28.1 0.0 collective-permute-done.4.near
  28.1 0.6 %collective-permute-done.5.far = f32[9,4,1152]{2,1,0:T(4,128)S(1)} collective-permute-done((f32[9,4,1152]{2,1,0:T(4,128)S(1)}, f32[9,4,1152]{2,1,0:T(4,128)S(1)}, u32[]{:S(2)}, u32[]{:S(2)}) %collective-permute-start.5) | collective-permute-done | bytes 165920 | tf_op jit(solution)/shard_map/ppermute | solution.py:441
  28.7 0.0 copy-done.1
  28.7 4.3 %shard_map.54 = (f32[32,32,384]{2,1,0:T(8,128)}, f32[3,1,1024]{2,1,0:T(1,128)}) custom-call(f32[9,4,1152]{2,1,0:T(4,128)S(1)} %collective-permute-done.4.near, f32[9,4,1152]{2,1,0:T(4,128)S(1)} %collective-permute-done.5.far, f32[1,4,1152]{2,1,0:T(4,128)S(1)} %bitcast.15, s32[3,1,1024]{2,1,0:T(1,128)S(1)} %bitcast.19, ...), custom_call_target="tpu_custom_call", output_to_operand_aliasing={{0}: (7, {})} | custom-call | tf_op jit(solution)/shard_map/pallas_call | solution.py:514
  (6 shorter events, 0.1 us)
Async XLA Ops:
  2.5 7.4 %collective-permute-start = (f32[1,4,1152]{2,1,0:T(4,128)S(1)}, f32[1,4,1152]{2,1,0:T(4,128)S(1)}, u32[]{:S(2)}, u32[]{:S(2)}) collective-permute-start(f32[1,4,1152]{2,1,0:T(4,128)S(1)} %bitcast.26), channel_id=1, source_target_pairs={{0,7},{1,2},{2,1},{3,4},{4,3},{5,6},{6,5},{7,0},{8,15},{9,10},{10,... | collective-permute-start | bytes 55304 | tf_op jit(solution)/shard_map/ppermute | solution.py:441
  7.1 5.3 %collective-permute-start.1 = (f32[1,4,1152]{2,1,0:T(4,128)S(1)}, f32[1,4,1152]{2,1,0:T(4,128)S(1)}, u32[]{:S(2)}, u32[]{:S(2)}) collective-permute-start(f32[1,4,1152]{2,1,0:T(4,128)S(1)} %bitcast.25), channel_id=1, source_target_pairs={{0,1},{1,0},{2,3},{3,2},{4,5},{5,4},{6,7},{7,6},{8,9},{9,8},{10,11... | collective-permute-start | bytes 55304 | tf_op jit(solution)/shard_map/ppermute | solution.py:441
  8.9 13.8 %copy-start = (s32[1,1,1,3,1024]{4,2,3,1,0:T(1,128)S(1)}, s32[1,1,1,3,1024]{4,2,3,1,0:T(1,128)}, u32[]{:S(2)}) copy-start(s32[1,1,1,3,1024]{4,2,3,1,0:T(1,128)} %param.4) | copy-start | bytes 36868
  12.4 4.2 %collective-permute-start.2 = (f32[3,4,1152]{2,1,0:T(4,128)S(1)}, f32[3,4,1152]{2,1,0:T(4,128)S(1)}, u32[]{:S(2)}, u32[]{:S(2)}) collective-permute-start(f32[3,4,1152]{2,1,0:T(4,128)S(1)} %get-tuple-element.26), channel_id=1, source_target_pairs={{0,192},{64,128},{128,64},{192,0},{1,193},{65,129},{129,65},{193,1... | collective-permute-start | bytes 165896 | tf_op jit(solution)/shard_map/ppermute | solution.py:441
  12.5 4.2 %collective-permute-start.3 = (f32[3,4,1152]{2,1,0:T(4,128)S(1)}, f32[3,4,1152]{2,1,0:T(4,128)S(1)}, u32[]{:S(2)}, u32[]{:S(2)}) collective-permute-start(f32[3,4,1152]{2,1,0:T(4,128)S(1)} %get-tuple-element.25), channel_id=1, source_target_pairs={{0,64},{64,0},{128,192},{192,128},{1,65},{65,1},{129,193},{193,129... | collective-permute-start | bytes 165896 | tf_op jit(solution)/shard_map/ppermute | solution.py:441
  16.7 11.9 %copy-start.1 = (f32[1,1,1,1024]{3,2,1,0:T(1,128)S(1)}, f32[1,1,1,1024]{3,2,1,0:T(1,128)}, u32[]{:S(2)}) copy-start(f32[1,1,1,1024]{3,2,1,0:T(1,128)} %param.3) | copy-start | bytes 12292
  16.8 11.3 %collective-permute-start.4 = (f32[9,4,1152]{2,1,0:T(4,128)S(1)}, f32[9,4,1152]{2,1,0:T(4,128)S(1)}, u32[]{:S(2)}, u32[]{:S(2)}) collective-permute-start(f32[9,4,1152]{2,1,0:T(4,128)S(1)} %constant_dynamic-update-slice_fusion.lists), channel_id=1, source_target_pairs={{0,56},{8,16},{16,8},{24,32},{32,24},{40,48},{48,40},{56,0},{1,57}... | collective-permute-start | bytes 497672 | tf_op jit(solution)/shard_map/ppermute | solution.py:441
  22.7 6.0 %collective-permute-start.5 = (f32[9,4,1152]{2,1,0:T(4,128)S(1)}, f32[9,4,1152]{2,1,0:T(4,128)S(1)}, u32[]{:S(2)}, u32[]{:S(2)}) collective-permute-start(f32[9,4,1152]{2,1,0:T(4,128)S(1)} %constant_dynamic-update-slice_fusion.lists), channel_id=1, source_target_pairs={{0,8},{8,0},{16,24},{24,16},{32,40},{40,32},{48,56},{56,48},{1,9},... | collective-permute-start | bytes 497672 | tf_op jit(solution)/shard_map/ppermute | solution.py:441
